TPU v7x, 32 devices: a whole 2x2x4 slice. The times are simulated.
32 devices in a mesh: row: 16 (over z, y, x), col: 2 (over core).
Axes of the slice: x: 2, y: 2, z: 4, core: 2. Of those that a mesh axis runs over, the one named last changes fastest.
Arguments:
- pair_trunk: bfloat16 [256, 256, 128], P('row', 'col'), may hold values from -6 to 6
- pair_gain: float32 [128], replicated, may hold values from 0.25 to 1.75
- pair_weight: bfloat16 [4, 128], replicated, may hold values from -0.5 to 0.5
- atom_features: bfloat16 [16, 2048, 128], P(None, ('row', 'col')), may hold values from -6 to 6
- atom_gain: float32 [128], replicated, may hold values from 0.25 to 1.75
- attn_weights: bfloat16 [4, 128, 128], replicated, may hold values from -0.5 to 0.5
- token_atoms: int32 [16, 16], replicated, may hold values from 1 to 24, 128 in all within a row
- window_starts: int32 [64], P(('row', 'col')), may hold values from 0 to 1920, as said below
- out_cotangent: bfloat16 [16, 2048, 128], P(None, ('row', 'col')), may hold values from -6 to 6
Outputs:
- updated: bfloat16 [16, 2048, 128], P(None, ('row', 'col'))
- grad_atoms: float32 [16, 2048, 128], P(None, ('row', 'col'))
- grad_pair: bfloat16 [256, 256, 128], P('row', 'col')
- grad_attn_weights: float32 [4, 128, 128], replicated
- grad_atom_gain: float32 [128], replicated
- grad_pair_weight: float32 [4, 128], replicated
- grad_pair_gain: float32 [128], replicated
Inputs may be any that keep to these rules, and one draw needn't show every extreme that they name: `window_starts`: query block b's window starts within 16 atoms of 32 * b + 32/2 - 128/2, clipped to the atoms; the first block's window starts at 0 and the last block's at 1920.
All inputs are finite; a program needn't handle non-finite values.
Results may differ from a plain program's by a relative error of at most 0.012.
Values may be sent and summed in bfloat16 or wider, within the bound.
A program may use at most 128 MiB of HBM per device.

v0:
```python
import math

import jax
import jax.numpy as jnp
from jax import lax
from jax.sharding import PartitionSpec as P

WINDOW = 128


def extended_2(block, sides, width):
    for axis, dim in sides:
        count = lax.axis_size(axis)
        forward = [(i, i + 1) for i in range(count - 1)]
        backward = [(target, source) for source, target in forward]
        low = lax.ppermute(
            lax.slice_in_dim(block, block.shape[dim] - width, None, axis=dim), axis, forward
        )
        high = lax.ppermute(lax.slice_in_dim(block, 0, width, axis=dim), axis, backward)
        block = jnp.concatenate([low, block, high], axis=dim)
    return block


def passed_along(block, axis, distance):
    devices = range(lax.axis_size(axis))
    route = [(i - distance, i) for i in devices if i - distance in devices]
    return lax.ppermute(block, axis, route)


def layer_norm(values, gain):
    center = values - jnp.mean(values, axis=-1, keepdims=True)
    spread = jnp.mean(center * center, axis=-1, keepdims=True)
    return center * lax.rsqrt(spread + 1e-05) * gain


def pair_norm(block, gain):
    return layer_norm(block.astype(jnp.float32), gain)


def pair_forward(pair_block, pair_gain, pair_weight):
    normed, norm_back = jax.vjp(pair_norm, pair_block, pair_gain)
    normed_bf = normed.astype(jnp.bfloat16)
    bias = jnp.einsum("ijc,hc->hij", normed_bf, pair_weight, preferred_element_type=jnp.float32)
    return (bias.astype(jnp.bfloat16), normed_bf, norm_back)


def pair_backward(grad_bias, normed_bf, pair_weight, norm_back):
    grad_weight = jnp.einsum(
        "hij,ijc->hc", grad_bias, normed_bf, preferred_element_type=jnp.float32
    )
    grad_normed = jnp.einsum(
        "hij,hc->ijc", grad_bias, pair_weight, preferred_element_type=jnp.float32
    )
    grad_block, grad_gain = norm_back(grad_normed)
    return (grad_block, grad_gain, grad_weight)


def project_atoms(atoms_f, atom_gain, attn_weights):
    normed, norm_back = jax.vjp(layer_norm, atoms_f, atom_gain)
    normed_bf = normed.astype(jnp.bfloat16)
    projected = jnp.einsum(
        "sac,pcd->psad", normed_bf, attn_weights[:3], preferred_element_type=jnp.float32
    ).astype(jnp.bfloat16)
    return (projected[0], projected[1:], normed_bf, norm_back)


def project_back(grad_proj, normed_bf, attn_weights, norm_back):
    grad_weight = jnp.einsum(
        "sac,psad->pcd", normed_bf, grad_proj, preferred_element_type=jnp.float32
    )
    grad_normed = jnp.einsum(
        "psad,pcd->sac", grad_proj, attn_weights[:3], preferred_element_type=jnp.float32
    )
    grad_in, grad_gain = norm_back(grad_normed)
    return (grad_in, grad_gain, grad_weight)


def block_attention(query_blk, keys_ext, offset, tile):
    heads = tile.shape[0]
    samples, rows_q, width = query_blk.shape
    head_dim = width // heads
    window = tile.shape[2]
    kv_win = lax.dynamic_slice_in_dim(keys_ext, offset, window, 2).astype(jnp.bfloat16)
    q_heads = query_blk.reshape(samples, rows_q, heads, head_dim)
    k_heads = kv_win[0].reshape(samples, window, heads, head_dim)
    v_heads = kv_win[1].reshape(samples, window, heads, head_dim)
    scores = (
        jnp.einsum("sqhd,skhd->shqk", q_heads, k_heads, preferred_element_type=jnp.float32)
        / math.sqrt(head_dim)
        + tile[None]
    )
    scores = scores - lax.stop_gradient(jnp.max(scores, axis=-1, keepdims=True))
    weights = jnp.exp(scores)
    probs = (weights / jnp.sum(weights, axis=-1, keepdims=True)).astype(jnp.bfloat16)
    mixed = jnp.einsum("shqk,skhd->sqhd", probs, v_heads, preferred_element_type=jnp.float32)
    return mixed.reshape(samples, rows_q, width).astype(jnp.bfloat16)


def device_attention(queries, keys_ext, offsets, tiles):
    samples, count, width = queries.shape
    nblk = offsets.shape[0]
    blocks = queries.reshape(samples, nblk, count // nblk, width)
    mixed = jax.vmap(block_attention, in_axes=(1, None, 0, 0), out_axes=1)(
        blocks, keys_ext, offsets, tiles
    )
    return mixed.reshape(samples, count, width)


def residual_out(mixed, atoms_f, attn_weights):
    moved = jnp.einsum("sac,cd->sad", mixed, attn_weights[3], preferred_element_type=jnp.float32)
    return (atoms_f + moved).astype(jnp.bfloat16)


def residual_back(cotangent, mixed, attn_weights):
    grad_weight = jnp.einsum("sac,sad->cd", mixed, cotangent, preferred_element_type=jnp.float32)
    grad_mixed = jnp.einsum(
        "sad,cd->sac", cotangent, attn_weights[3], preferred_element_type=jnp.float32
    )
    return (grad_mixed.astype(jnp.bfloat16), grad_weight)


def token_index(atom_ids, token_atoms, band_atoms):
    band_id = atom_ids // band_atoms
    local_id = atom_ids - band_id * band_atoms
    totals = jnp.cumsum(token_atoms, axis=1)
    rows_sel = totals[band_id]
    found = jnp.sum((rows_sel <= local_id[..., None]).astype(jnp.int32), axis=-1)
    return band_id * token_atoms.shape[1] + found


def per_device(
    pair_trunk,
    pair_gain,
    pair_weight,
    atom_features,
    atom_gain,
    attn_weights,
    token_atoms,
    window_starts,
    out_cotangent,
):
    row_index = lax.axis_index("row")
    col_index = lax.axis_index("col")
    col_count = lax.axis_size("col")
    band_rows = pair_trunk.shape[0]
    col_width = pair_trunk.shape[1]
    total_tokens = col_width * col_count
    samples, atom_count, width = atom_features.shape
    half = WINDOW // 2
    first_atom = (row_index * col_count + col_index) * atom_count
    atoms_f = atom_features.astype(jnp.float32)
    bias_own, pair_normed, pair_norm_back = pair_forward(pair_trunk, pair_gain, pair_weight)
    heads = bias_own.shape[0]
    span = band_rows + WINDOW
    window_first = jnp.clip(row_index * band_rows - half, 0, total_tokens - span)
    band_bias = lax.all_gather(bias_own, "col", axis=2, tiled=True)
    window_bias = lax.dynamic_slice_in_dim(band_bias, window_first, span, 2).astype(jnp.float32)
    band_atoms = atom_count * col_count
    query_ids = first_atom + jnp.arange(atom_count, dtype=jnp.int32)
    query_tok = (token_index(query_ids, token_atoms, band_atoms) - row_index * band_rows).reshape(
        window_starts.shape[0], atom_count // window_starts.shape[0]
    )
    key_ids = window_starts[:, None] + jnp.arange(WINDOW, dtype=jnp.int32)[None, :]
    key_tok = token_index(key_ids, token_atoms, band_atoms) - window_first
    offsets = window_starts - (first_atom - half)
    queries, keyvals, atom_normed, atom_norm_back = project_atoms(atoms_f, atom_gain, attn_weights)
    extended = extended_2(keyvals, ((("row", "col"), 2),), half).astype(jnp.float32)

    def attend(query_in, keys_ext, bias_window):
        tiles = bias_window[:, query_tok[:, :, None], key_tok[:, None, :]].transpose(1, 0, 2, 3)
        return device_attention(query_in, keys_ext, offsets, tiles)

    mixed, attend_back = jax.vjp(attend, queries, extended, window_bias)
    updated = residual_out(mixed, atoms_f, attn_weights)
    grad_mixed, grad_w_out = residual_back(out_cotangent, mixed, attn_weights)
    grad_queries, grad_ext, grad_window = attend_back(grad_mixed)
    lower_rim = grad_ext[:, :, :half]
    upper_rim = grad_ext[:, :, half + atom_count :]
    inner_grad = grad_ext[:, :, half : half + atom_count]
    from_below = passed_along(upper_rim.astype(jnp.bfloat16), ("row", "col"), 1).astype(
        upper_rim.dtype
    )
    from_above = passed_along(lower_rim.astype(jnp.bfloat16), ("row", "col"), -1).astype(
        lower_rim.dtype
    )
    inner_grad = inner_grad.at[:, :, :half].add(from_below)
    inner_grad = inner_grad.at[:, :, atom_count - half :].add(from_above)
    grad_proj = jnp.concatenate([grad_queries[None], inner_grad.astype(jnp.bfloat16)], axis=0)
    grad_in, grad_atom_gain, grad_w_proj = project_back(
        grad_proj, atom_normed, attn_weights, atom_norm_back
    )
    spread_grad = lax.dynamic_update_slice_in_dim(
        jnp.zeros((heads, band_rows, total_tokens), jnp.float32), grad_window, window_first, 2
    )
    grad_own = lax.psum_scatter(
        spread_grad.astype(jnp.bfloat16), "col", scatter_dimension=2, tiled=True
    )
    grad_pair, grad_pair_gain, grad_pair_weight = pair_backward(
        grad_own, pair_normed, pair_weight, pair_norm_back
    )
    grad_weights = jnp.concatenate([grad_w_proj, grad_w_out[None]], axis=0)
    totals = lax.psum(
        (grad_weights, grad_atom_gain, grad_pair_weight, grad_pair_gain), ("row", "col")
    )
    grad_atoms = out_cotangent.astype(jnp.float32) + grad_in
    return (updated, grad_atoms, grad_pair, totals[0], totals[1], totals[2], totals[3])


def solution(mesh):
    placed = (
        P("row", "col", None),
        P(),
        P(),
        P(None, ("row", "col"), None),
        P(),
        P(),
        P(),
        P(("row", "col")),
        P(None, ("row", "col"), None),
    )
    return jax.shard_map(
        per_device,
        mesh=mesh,
        in_specs=placed,
        out_specs=(
            P(None, ("row", "col"), None),
            P(None, ("row", "col"), None),
            P("row", "col", None),
            P(),
            P(),
            P(),
            P(),
        ),
        check_vma=False,
    )
```

profile of v0, /device:TPU:0, one launch (start us, length us, event | category | flops | bytes accessed | tf_op | source)
XLA Modules:
  0.0 419.7 jit_solution(5552119893999655951)
XLA Ops:
  9.3 1.3 fusion.45
  10.7 1.5 fusion.23
  12.3 1.4 collective-permute-start.1
  13.7 3.9 collective-permute-start
  22.0 3.2 all_gather.3
  25.6 1.3 copy.184
  27.0 1.4 copy.131
  28.9 88.5 %gather_fusion.3 = f32[8192,4]{1,0:T(8,128)} fusion(f32[4,16,144]{0,2,1:T(8,128)S(1)} %copy.128, s32[8192]{0:T(1024)S(1)} %bitcast.126), kind=kCustom, calls=%fused_computation.3 | custom fusion | bytes 327680 | tf_op jit(solution)/shard_map/jvp()/gather | solution.py:170
  117.3 2.9 copy.129
  121.8 1.3 maximum_convert_fusion
  124.1 2.2 gather_fusion
  126.3 1.9 fusion.90
  128.2 1.7 copy.123
  129.9 1.7 copy.121
  131.6 3.1 fusion.92
  134.7 3.1 convolution_convert_fusion
  137.9 1.7 fusion.4
  139.7 2.3 fusion.13
  142.0 2.3 fusion.16
  144.3 1.3 fusion.86
  145.5 1.8 convolution_convert_fusion.2
  147.3 1.6 copy.137
  149.0 1.7 copy.139
  150.6 1.6 copy.130
  152.2 1.7 fusion.24
  153.9 2.2 add_convert_fusion
  156.1 2.0 broadcast_in_dim.33.clone
  158.1 38.4 %while.5 = (s32[]{:T(128)}, f32[2,16,192,128]{3,2,0,1:T(8,128)}, s32[2,4]{1,0:T(2,128)}, f32[2,2,16,128,128]{4,3,2,1,0:T(8,128)}, s32[]{:T(128)}, /*index=5*/s32[4]{0:T(128)S(1)}, s32[]{:T(128)}) while((s32[]{:T(128)}, f32[2,16,192,128]{3,2,0,1:T(8,128)}, s32[2,4]{1,0:T(2,128)}, f32[2,2,16,128,128]{4,3,2,1,0:T(8,128)}, s32[]{:T(128)}, ...), condition=%wide.while_cond.2, body=%wide.while_body.2.sunk | while | flops 1048605 | bytes 14681282 | solution.py:83
  159.5 3.3 and_reduce_fusion.2
  162.7 3.8 add_select_fusion.2
  166.8 10.6 %dynamic-update-slice.7 = f32[2,16,192,128]{3,2,0,1:T(8,128)} dynamic-update-slice(f32[2,16,192,128]{3,2,0,1:T(8,128)} %get-tuple-element.168, f32[2,16,128,128]{3,2,0,1:T(8,128)S(1)} %copy.194, s32[]{:T(128)} %constant.151.clone.1..sunk, s32[]{:T(128)} %constant.151.clone.1..sunk, s32[]{:T(128)} %bitcast.125, s32[]{:T(128)} %constant.151.clone.1..sunk) | dynamic-update-slice | bytes 4194308 | tf_op jit(solution)/shard_map/transpose(jvp(vmap()))/scatter-add
  178.7 3.3 and_reduce_fusion.2
  182.0 3.8 add_select_fusion.2
  186.0 10.6 %dynamic-update-slice.7 = f32[2,16,192,128]{3,2,0,1:T(8,128)} dynamic-update-slice(f32[2,16,192,128]{3,2,0,1:T(8,128)} %get-tuple-element.168, f32[2,16,128,128]{3,2,0,1:T(8,128)S(1)} %copy.194, s32[]{:T(128)} %constant.151.clone.1..sunk, s32[]{:T(128)} %constant.151.clone.1..sunk, s32[]{:T(128)} %bitcast.125, s32[]{:T(128)} %constant.151.clone.1..sunk) | dynamic-update-slice | bytes 4194308 | tf_op jit(solution)/shard_map/transpose(jvp(vmap()))/scatter-add
  196.6 2.1 convert.4
  199.6 2.6 copy.155
  202.2 52.8 %scatter_custom_fusion = f32[4,2304]{0,1:T(8,128)S(1)} fusion(s32[8192]{0:T(1024)} %bitcast.154, f32[8192,4]{1,0:T(8,128)} %bitcast.129, f32[]{:T(128)} %constant.148.clone.1), kind=kCustom, calls=%fused_computation.70 | custom fusion | flops 32768 | bytes 37376
  257.0 1.8 reshape.516
  259.1 1.8 copy.133
  261.4 3.2 collective-permute-start.2
  264.7 1.3 collective-permute-start.3
  266.0 5.7 %reduce-scatter.4.cloned.1.call-done = bf16[128,64]{1,0:T(8,128)(2,1)} async-done(((bf16[256,64]{1,0:T(8,128)(2,1)}), bf16[128,64]{1,0:T(8,128)(2,1)}) %reduce-scatter.4.cloned.1.call-update) | async-done | bytes 16400
  271.6 1.4 reshape.517
  276.5 1.5 add_convert_fusion.2
  280.7 1.4 add_add_fusion.2
  282.1 46.0 %all-reduce.2 = (f32[128]{0:T(128)}, f32[4,128]{1,0:T(4,128)}, f32[128]{0:T(128)}) all-reduce(f32[128]{0:T(128)S(1)} %get-tuple-element.92, f32[4,128]{1,0:T(4,128)S(1)} %convolution_bitcast_fusion.3, f32[128]{0:T(128)S(1)} %get-tuple-element.90), channel_id=1, replica_groups=mesh['row'=16,'col'=2] {'row','col'}, use_global_device_ids=true, to_apply=%region_20.21 | all-reduce | flops 768 | bytes 6144 | tf_op jit(solution)/shard_map/psum | solution.py:202
  328.1 82.4 %all-reduce.5.cloned.1.call-done = f32[4,128,128]{1,2,0:T(8,128)} async-done(((f32[4,128,128]{1,2,0:T(8,128)}), f32[4,128,128]{1,2,0:T(8,128)}) %all-reduce.5.cloned.1.call-update) | async-done | bytes 262160 | tf_op jit(solution)/shard_map/psum | solution.py:202
  410.5 1.8 copy.148
  (137 shorter events, 21.9 us)
Async XLA Ops:
  8.0 13.4 %copy-start = (bf16[4,128]{1,0:T(4,128)(2,1)S(1)}, bf16[4,128]{1,0:T(4,128)(2,1)}, u32[]{:S(2)}) copy-start(bf16[4,128]{1,0:T(4,128)(2,1)} %param.19) | copy-start | bytes 3076
  8.0 9.6 %copy-start.25 = (s32[2]{0:T(128)S(1)}, s32[2]{0:T(128)}, u32[]{:S(2)}) copy-start(s32[2]{0:T(128)} %param.24) | copy-start | bytes 28
  8.0 9.9 %copy-start.21 = (s32[16,16]{1,0:T(8,128)S(1)}, s32[16,16]{1,0:T(8,128)}, u32[]{:S(2)}) copy-start(s32[16,16]{1,0:T(8,128)} %param.23) | copy-start | bytes 3076
  8.0 263.6 %reduce-scatter.4.cloned.1.call-start = ((), (), s32[]{:S(2)}) async-start(), calls=%async_computation.2 | async-start | bytes 98304
  9.3 8.7 %copy-start.9 = (f32[16,64]{1,0:T(8,128)}, f32[16,64]{1,0:T(8,128)S(1)}, u32[]{:S(2)}) copy-start(f32[16,64]{1,0:T(8,128)S(1)} %broadcast_multiply_fusion.1) | copy-start | bytes 12292
  10.6 9.2 %copy-start.18 = (f32[16,64]{1,0:T(8,128)}, f32[16,64]{1,0:T(8,128)S(1)}, u32[]{:S(2)}) copy-start(f32[16,64]{1,0:T(8,128)S(1)} %fusion.45) | copy-start | bytes 12292
  10.6 9.1 %copy-start.12 = (f32[16,64]{1,0:T(8,128)}, f32[16,64]{1,0:T(8,128)S(1)}, u32[]{:S(2)}) copy-start(f32[16,64]{1,0:T(8,128)S(1)} %fusion.70) | copy-start | bytes 12292
  10.6 9.1 %copy-start.7 = (bf16[16,64,128]{2,1,0:T(8,128)(2,1)S(1)}, bf16[16,64,128]{2,1,0:T(8,128)(2,1)}, u32[]{:S(2)}) copy-start(bf16[16,64,128]{2,1,0:T(8,128)(2,1)} %param.25) | copy-start | bytes 786436
  12.2 8.9 %copy-start.6 = (bf16[3,16,64,128]{3,2,0,1:T(8,128)(2,1)}, bf16[3,16,64,128]{3,2,0,1:T(8,128)(2,1)S(1)}, u32[]{:S(2)}) copy-start(bf16[3,16,64,128]{3,2,0,1:T(8,128)(2,1)S(1)} %fusion.23) | copy-start | bytes 2359300
  12.2 8.6 %copy-start.8 = (bf16[16,128,128]{2,1,0:T(8,128)(2,1)S(1)}, bf16[16,128,128]{2,1,0:T(8,128)(2,1)}, u32[]{:S(2)}) copy-start(bf16[16,128,128]{2,1,0:T(8,128)(2,1)} %param.17) | copy-start | bytes 1572868
  12.3 109.5 %collective-permute-start.1 = (bf16[2,16,64,128]{3,2,0,1:T(8,128)(2,1)S(1)}, bf16[2,16,64,128]{3,2,0,1:T(8,128)(2,1)}, u32[]{:S(2)}, u32[]{:S(2)}) collective-permute-start(bf16[2,16,64,128]{3,2,0,1:T(8,128)(2,1)S(1)} %slice.123), channel_id=1, source_target_pairs={{1,0},{2,1},{3,2},{4,3},{5,4},{6,5},{7,6},{8,7},{9,8},{10,9},{11,1... | collective-permute-start | bytes 1572872 | tf_op jit(solution)/shard_map/ppermute | solution.py:19
  13.7 108.1 %collective-permute-start = (bf16[2,16,64,128]{3,2,0,1:T(8,128)(2,1)S(1)}, bf16[2,16,64,128]{3,2,0,1:T(8,128)(2,1)}, u32[]{:S(2)}, u32[]{:S(2)}) collective-permute-start(bf16[2,16,64,128]{3,2,0,1:T(8,128)(2,1)S(1)} %slice.123), channel_id=1, source_target_pairs={{0,1},{1,2},{2,3},{3,4},{4,5},{5,6},{6,7},{7,8},{8,9},{9,10},{10,1... | collective-permute-start | bytes 1572872 | tf_op jit(solution)/shard_map/ppermute | solution.py:16
  18.1 3.3 copy-start.22
  21.2 4.4 %slice-start = ((bf16[3,16,64,128]{3,2,0,1:T(8,128)(2,1)}), bf16[1,16,64,128]{3,2,0,1:T(8,128)(2,1)S(1)}, s32[]{:S(2)}) async-start(bf16[3,16,64,128]{3,2,0,1:T(8,128)(2,1)} %copy-done.6), calls=%async_computation.3 | async-start | bytes 524288 | tf_op jit(solution)/shard_map/slice | solution.py:64
  21.4 0.6 copy-start.16
  21.4 0.6 copy-start.14
  117.3 3.0 copy-start.27
  117.3 3.1 copy-start.26
  117.3 3.2 copy-start.20
  134.7 3.2 copy-start.3
  134.7 3.1 copy-start.4
  137.9 1.8 copy-start.2
  139.6 2.3 copy-start.5
  149.0 3.3 copy-start.1
  258.7 151.7 %all-reduce.5.cloned.1.call-start = ((), (), s32[]{:S(2)}) async-start(), calls=%async_computation.1 | async-start | bytes 524288 | tf_op jit(solution)/shard_map/psum | solution.py:202
  259.1 14.4 %copy-start.23 = (f32[128]{0:T(128)S(1)}, f32[128]{0:T(128)}, u32[]{:S(2)}) copy-start(f32[128]{0:T(128)} %param.18) | copy-start | bytes 1540
  260.9 13.0 %copy-start.17 = (f32[16,128]{1,0:T(8,128)S(1)}, f32[16,128]{1,0:T(8,128)}, u32[]{:S(2)}) copy-start(f32[16,128]{1,0:T(8,128)} %copy-done.16) | copy-start | bytes 24580
  260.9 13.0 %copy-start.15 = (f32[16,128]{1,0:T(8,128)S(1)}, f32[16,128]{1,0:T(8,128)}, u32[]{:S(2)}) copy-start(f32[16,128]{1,0:T(8,128)} %copy-done.14) | copy-start | bytes 24580
  261.4 15.1 %collective-permute-start.2 = (bf16[2,16,64,128]{3,2,0,1:T(8,128)(2,1)}, bf16[2,16,64,128]{3,2,0,1:T(8,128)(2,1)S(1)}, u32[]{:S(2)}, u32[]{:S(2)}) collective-permute-start(bf16[2,16,64,128]{3,2,0,1:T(8,128)(2,1)} %get-tuple-element.117), channel_id=1, source_target_pairs={{0,1},{1,2},{2,3},{3,4},{4,5},{5,6},{6,7},{7,8},{8,9},{9,10},{10,1... | collective-permute-start | bytes 1572872 | tf_op jit(solution)/shard_map/ppermute | solution.py:27
  264.7 11.8 %collective-permute-start.3 = (bf16[2,16,64,128]{3,2,0,1:T(8,128)(2,1)S(1)}, bf16[2,16,64,128]{3,2,0,1:T(8,128)(2,1)S(1)}, u32[]{:S(2)}, u32[]{:S(2)}) collective-permute-start(bf16[2,16,64,128]{3,2,0,1:T(8,128)(2,1)S(1)} %get-tuple-element.118), channel_id=1, source_target_pairs={{1,0},{2,1},{3,2},{4,3},{5,4},{6,5},{7,6},{8,7},{9,8},{10,9},{11,1... | collective-permute-start | bytes 1572872 | tf_op jit(solution)/shard_map/ppermute | solution.py:27
  275.1 2.9 copy-start.10
  275.1 2.9 copy-start.13
  275.1 2.9 copy-start.24
  276.5 2.3 copy-start.11
  278.1 1.2 copy-start.19
Sparse Core Ops, SparseCore 0:
  258.9 12.7 reduce-scatter.3
Sparse Core Ops, SparseCore 1:
  280.1 130.3 all-reduce.4
where the time goes:
time: 422 us; the launch traced here: 420 us
  local copies, waits for them, and re-layouts  151 us (36%)
  waiting for transfers between devices  88.1 us (21%)
  other arithmetic  84.6 us (20%)
  blocking collectives  49.2 us (12%)
  matrix products  21 us (5%)
  between operations  16.2 us (4%)
  starting transfers between devices  9.88 us (2%)
    gather x2, local copies, waits for them, and re-layouts, attend(): bias_window[:, query_tok[:, :, None], key_tok[:, None, :]]  91.3 us
    psum x1, waiting for transfers between devices, per_device(): lax.psum((grad_weights, grad_atom_gain, grad_pair_weight, grad_pair_gain)...  82.4 us
    unnamed x4, other arithmetic  53.6 us
    psum x1, blocking collectives, per_device(): lax.psum((grad_weights, grad_atom_gain, grad_pair_weight, grad_pair_gain)...  46 us
    scatter-add x8, local copies, waits for them, and re-layouts  24.2 us
    scatter-add x4, other arithmetic  14.2 us
  transfers between devices with their start and end apart: 6, of which 2 were waited for; matrix products, arithmetic and copies ran while one was open for 26% of the time, Pallas kernels for 0%

commit v1 on v0

v1 whole, which is shorter than its diff:
```python
import functools
import math

import jax
import jax.numpy as jnp
from jax import lax
from jax.experimental import pallas as pl
from jax.experimental.pallas import tpu as pltpu
from jax.sharding import PartitionSpec as P

WINDOW = 128
EPS = 1e-05
MESH = pl.DeviceIdType.MESH
F32 = jnp.float32
BF16 = jnp.bfloat16
NT = (((1,), (1,)), ((), ()))
NN = (((1,), (0,)), ((), ()))
TN = (((0,), (0,)), ((), ()))
MASKED = -1e30
GROUP = 4
PAIRED = 2


def dot(a, b, dims):
    return lax.dot_general(a, b, dims, preferred_element_type=F32)


def iota(shape, dim):
    return lax.broadcasted_iota(jnp.int32, shape, dim)


def normalised(x):
    x = x.astype(F32)
    center = x - jnp.mean(x, axis=-1, keepdims=True)
    rstd = lax.rsqrt(jnp.mean(center * center, axis=-1, keepdims=True) + EPS)
    return center * rstd, rstd


def norm_back(grad, gain, xhat, rstd):
    scaled = grad * gain
    first = jnp.mean(scaled, axis=-1, keepdims=True)
    second = jnp.mean(scaled * xhat, axis=-1, keepdims=True)
    return rstd * (scaled - first - xhat * second)


def fold8(x):
    return jnp.sum(x.reshape(x.shape[0] // 8, 8, x.shape[1]), axis=0)


def kernel(
    n_row, n_col,
    trunk, pair_gain, pair_weight, atoms, atom_gain, weights, token_atoms, starts, cot,
    updated, grad_atoms, grad_pair, grad_w, grad_again, grad_pweight, grad_pgain,
    halo, q_s, k_ext, v_ext, n_ext, xhat_s, rstd_s, gmix, mixed_s, dq_s, dkv_s,
    dn_own, dn_out, dn_in, tile, dt_acc, ok_s, oq_s, hmask_s, wrep_s, pxhat, prstd,
    bias_all, g_out, g_in, rs_out, rs_in, cb, ag, sm, sc,
    halo_ss, halo_rs, bias_ss, bias_rs, dn_ss, dn_rs, g_ss, g_rs,
    rs_ss, rs_rs, cb_ss, cb_rs, ag_ss, ag_rs, sm_ss, sm_rs, sc_ss, sc_rs,
):
    row = lax.axis_index("row")
    col = lax.axis_index("col")
    n_dev = n_row * n_col
    me = row * n_col + col
    up = lax.rem(me + 1, n_dev)
    down = lax.rem(me + n_dev - 1, n_dev)
    up_id = (up // n_col, lax.rem(up, n_col))
    down_id = (down // n_col, lax.rem(down, n_col))
    samples, count, width = atoms.shape
    band, cols, _ = trunk.shape
    heads = pair_weight.shape[0]
    head_dim = width // heads
    total = cols * n_col
    lanes = wrep_s.shape[0]
    ext = count + WINDOW
    half = WINDOW // 2
    hq = heads * count
    scale = 1.0 / math.sqrt(head_dim)
    band_atoms = count * n_col
    first = me * count

    def row_peer(d):
        return lax.rem(row + d, n_row)

    def col_peer(d):
        return lax.rem(col + d, n_col)

    barrier = pltpu.get_barrier_semaphore()
    pl.semaphore_signal(barrier, inc=1, device_id=up_id, device_id_type=MESH)
    pl.semaphore_signal(barrier, inc=1, device_id=down_id, device_id_type=MESH)

    @pl.loop(1, n_row)
    def _(d):
        pl.semaphore_signal(barrier, inc=1, device_id=(row_peer(d), col), device_id_type=MESH)

    @pl.loop(1, n_col)
    def _(d):
        pl.semaphore_signal(barrier, inc=1, device_id=(row, col_peer(d)), device_id_type=MESH)

    again = atom_gain[...]
    pgain = pair_gain[...]

    wqkv = jnp.concatenate([weights[0], weights[1], weights[2]], axis=1)
    wkv = jnp.concatenate([weights[1], weights[2]], axis=1)

    @pl.loop(0, samples // GROUP)
    def _(c):
        some = pl.ds(c * GROUP, GROUP)
        flat = (GROUP * count, width)
        cube = (GROUP, count, width)
        xhat, rstd = normalised(atoms[some].reshape(flat))
        normed = (xhat * again).astype(BF16)
        proj = dot(normed, wqkv, NN).astype(BF16)
        xhat_s[some] = xhat.reshape(cube)
        rstd_s[some] = rstd.reshape(GROUP, count, 1)
        n_ext[some, half : half + count] = normed.reshape(cube)
        q_s[some] = proj[:, :width].reshape(cube)
        k_ext[some, half : half + count] = proj[:, width : 2 * width].reshape(cube)
        v_ext[some, half : half + count] = proj[:, 2 * width :].reshape(cube)
        gmix[some] = dot(cot[some].reshape(flat), weights[3], NT).astype(BF16).reshape(cube)

    pl.semaphore_wait(barrier, n_row + n_col)

    def halo_copy(d, where):
        return pltpu.make_async_remote_copy(
            src_ref=atoms, dst_ref=halo.at[d], send_sem=halo_ss.at[d], recv_sem=halo_rs.at[d],
            device_id=where, device_id_type=MESH)

    halos = [halo_copy(0, up_id), halo_copy(1, down_id)]
    for copy in halos:
        copy.start()

    lane_row = iota((lanes, width), 0)
    wrep = jnp.zeros((lanes, width), F32)
    for h in range(heads):
        wrep = jnp.where(lane_row // band == h, pair_weight[h : h + 1, :].astype(F32), wrep)
    wrep_s[...] = wrep.astype(BF16)

    def pair_rows(i):
        return jnp.where(lane_row % band == i, wrep_s[...].astype(F32), 0.0).astype(BF16)

    def forward_step(i, acc):
        xhat, rstd = normalised(trunk[i])
        pxhat[i] = xhat
        prstd[i] = rstd
        return acc + dot((xhat * pgain).astype(BF16), pair_rows(i), NT)

    bias = lax.fori_loop(0, band, forward_step, jnp.zeros((cols, lanes), F32), unroll=2)
    bias_all[col] = bias.astype(BF16)

    def bias_copy(peer, slot):
        return pltpu.make_async_remote_copy(
            src_ref=bias_all.at[col], dst_ref=bias_all.at[slot], send_sem=bias_ss.at[peer],
            recv_sem=bias_rs.at[slot], device_id=(row, peer), device_id_type=MESH)

    @pl.loop(1, n_col)
    def _(d):
        bias_copy(col_peer(d), col).start()

    table = token_atoms[...].astype(F32).astype(BF16)

    def bounds(size, token_of, band_of, band_row):
        token = token_of(iota((band, size), 1))
        at = iota((band, size), 0)
        own = iota((n_row, size), 0) == band_of(iota((n_row, size), 1))
        out = []
        for strict in (True, False):
            below = (at < token) if strict else (at <= token)
            sums = dot(table, jnp.where(below, 1.0, 0.0).astype(BF16), NN)
            inner = jnp.sum(jnp.where(own, sums, 0.0), axis=0, keepdims=True)
            out.append(inner.astype(jnp.int32) + band_row(iota((1, size), 1)) * band_atoms)
        return out

    low, high = bounds(total, lambda j: j % band, lambda j: j // band, lambda j: j // band)
    key_atom = first - half + iota((ext, total), 0)
    ok_s[...] = jnp.where((key_atom >= low) & (key_atom < high), 1.0, 0.0).astype(BF16)
    low, high = bounds(lanes, lambda l: l % band, lambda l: l * 0 + row, lambda l: l * 0 + row)
    sub = iota((hq, lanes), 0)
    query_atom = first + sub % count
    same_head = (sub // count) == (iota((hq, lanes), 1) // band)
    oq_s[...] = jnp.where(
        same_head & (query_atom >= low) & (query_atom < high), 1.0, 0.0).astype(BF16)
    hmask_s[...] = jnp.where(
        iota((hq, width), 0) // count == iota((hq, width), 1) // head_dim, 1.0, 0.0).astype(BF16)

    for d, copy in enumerate(halos):
        copy.wait()
        base = d * (half + count)

        @pl.loop(0, samples // GROUP)
        def _(c, d=d, base=base):
            some = pl.ds(c * GROUP, GROUP)
            cube = (GROUP, half, width)
            side = halo[d, some]
            xhat, _r = normalised(side.reshape(GROUP * half, width))
            normed = (xhat * again).astype(BF16)
            proj = dot(normed, wkv, NN).astype(BF16)
            n_ext[some, base : base + half] = normed.reshape(cube)
            k_ext[some, base : base + half] = proj[:, :width].reshape(cube)
            v_ext[some, base : base + half] = proj[:, width:].reshape(cube)

    @pl.loop(1, n_col)
    def _(d):
        peer = col_peer(d)
        bias_copy(peer, peer).wait()

    spread = dot(ok_s[...], bias_all[...].reshape(total, lanes), NN).astype(BF16)
    block = (iota((ext, hq), 1) % count) // (count // starts.shape[0])
    offset = jnp.zeros((ext, hq), jnp.int32)
    for b in range(starts.shape[0]):
        offset = jnp.where(block == b, starts[b] - (first - half), offset)
    place = iota((ext, hq), 0) - offset
    tile[...] = jnp.where(
        (place >= 0) & (place < WINDOW), dot(spread, oq_s[...], NT), MASKED)
    dt_acc[...] = jnp.zeros_like(dt_acc)

    def dn_copy(d, it, where):
        some = pl.ds(it * PAIRED, PAIRED)
        return pltpu.make_async_remote_copy(
            src_ref=dn_out.at[d, some], dst_ref=dn_in.at[d, some], send_sem=dn_ss.at[d, it],
            recv_sem=dn_rs.at[d, it], device_id=where, device_id_type=MESH)

    def by_head(full):
        masked = full * hmask_s[...].astype(F32)
        out = masked[:count]
        for h in range(1, heads):
            out = out + masked[h * count : (h + 1) * count]
        return out

    def spread_heads(x):
        return jnp.concatenate([x] * heads, axis=0) * hmask_s[...]

    @pl.loop(0, samples // PAIRED)
    def _(it):
        added = None
        for u in range(PAIRED):
            s = it * PAIRED + u
            k, v = k_ext[s], v_ext[s]
            qbd = spread_heads(q_s[s])
            gbd = spread_heads(gmix[s])
            scores = dot(k, qbd, NT) * scale + tile[...]
            grown = jnp.exp(scores - jnp.max(scores, axis=0, keepdims=True))
            probs = grown * (1.0 / jnp.sum(grown, axis=0, keepdims=True))
            probs_bf = probs.astype(BF16)
            mixed_s[s] = by_head(dot(probs_bf, v, TN)).astype(BF16)
            gprobs = dot(v, gbd, NT).astype(BF16).astype(F32)
            weighed = probs * gprobs
            gscores = weighed - probs * jnp.sum(weighed, axis=0, keepdims=True)
            added = gscores if added is None else added + gscores
            gs_bf = (gscores * scale).astype(BF16)
            gq = by_head(dot(gs_bf, k, TN)).astype(BF16)
            gk = dot(gs_bf, qbd, NN).astype(BF16)
            gv = dot(probs_bf, gbd, NN).astype(BF16)
            dq_s[s] = gq
            dkv_s[s, :, :width] = gk
            dkv_s[s, :, width:] = gv
            gn = dot(gk, weights[1], NT) + dot(gv, weights[2], NT)
            dn_out[0, s] = gn[:half].astype(BF16)
            dn_out[1, s] = gn[half + count :].astype(BF16)
            dn_own[s] = gn[half : half + count] + dot(gq, weights[0], NT)
        dt_acc[...] += added
        dn_copy(0, it, down_id).start()
        dn_copy(1, it, up_id).start()

    by_query = dot(dt_acc[...].astype(BF16), oq_s[...], NN).astype(BF16)
    g_out[...] = dot(ok_s[...], by_query, TN).astype(BF16).reshape(n_col, cols, lanes)

    def g_copy(peer, slot):
        return pltpu.make_async_remote_copy(
            src_ref=g_out.at[peer], dst_ref=g_in.at[slot], send_sem=g_ss.at[peer],
            recv_sem=g_rs.at[slot], device_id=(row, peer), device_id_type=MESH)

    @pl.loop(1, n_col)
    def _(d):
        g_copy(col_peer(d), col).start()

    g_in[col] = g_out[col]

    rows_all = samples * count
    share = rs_out.shape[1]
    own_n = n_ext[:, half : half + count].reshape(rows_all, width)
    per = width // share
    gwq = dot(own_n, dq_s[...].reshape(rows_all, width), TN)
    gwkv = dot(n_ext[...].reshape(samples * ext, width),
               dkv_s[...].reshape(samples * ext, 2 * width), TN)
    mixed_all = mixed_s[...].reshape(rows_all, width)
    gwo = dot(mixed_all, cot[...].reshape(rows_all, width), TN)
    for p, value in enumerate((gwq, gwkv[:, :width], gwkv[:, width:], gwo)):
        rs_out[p * per : (p + 1) * per] = value.astype(BF16).reshape(per, share, width)

    def rs_copy(peer, slot):
        return pltpu.make_async_remote_copy(
            src_ref=rs_out.at[peer], dst_ref=rs_in.at[slot], send_sem=rs_ss.at[peer],
            recv_sem=rs_rs.at[slot], device_id=(peer, col), device_id_type=MESH)

    @pl.loop(1, n_row)
    def _(d):
        rs_copy(row_peer(d), row).start()

    rs_in[row] = rs_out[row]

    @pl.loop(0, samples // GROUP)
    def _(c):
        some = pl.ds(c * GROUP, GROUP)
        moved = dot(mixed_s[some].reshape(GROUP * count, width), weights[3], NN)
        updated[some] = (atoms[some].astype(F32) + moved.reshape(GROUP, count, width)).astype(BF16)

    @pl.loop(1, n_col)
    def _(d):
        peer = col_peer(d)
        g_copy(peer, peer).wait()

    grad_bias = g_in[0].astype(F32)
    for c in range(1, n_col):
        grad_bias = grad_bias + g_in[c].astype(F32)
    grad_bias_t = grad_bias.T.astype(BF16)
    grad_bias = grad_bias.astype(BF16)

    def backward_step(i, carry):
        gain_acc, w_acc = carry
        xhat = pxhat[i]
        grad = dot(grad_bias, pair_rows(i), NN)
        normed = (xhat * pgain).astype(BF16)
        gain_acc = gain_acc + fold8(grad * xhat)
        w_acc = w_acc + jnp.where(lane_row % band == i, dot(grad_bias_t, normed, NN), 0.0)
        grad_pair[i] = norm_back(grad, pgain, xhat, prstd[i]).astype(BF16)
        return gain_acc, w_acc

    pgain_acc, w_acc = lax.fori_loop(
        0, band, backward_step,
        (jnp.zeros((8, width), F32), jnp.zeros((lanes, width), F32)), unroll=2)

    @pl.loop(1, n_row)
    def _(d):
        peer = row_peer(d)
        rs_copy(peer, peer).wait()

    part = rs_in[0].astype(F32)
    for r in range(1, n_row):
        part = part + rs_in[r].astype(F32)
    cb[col] = part

    def cb_copy(peer, slot):
        return pltpu.make_async_remote_copy(
            src_ref=cb.at[col], dst_ref=cb.at[slot], send_sem=cb_ss.at[peer],
            recv_sem=cb_rs.at[slot], device_id=(row, peer), device_id_type=MESH)

    @pl.loop(1, n_col)
    def _(d):
        cb_copy(col_peer(d), col).start()

    @pl.loop(0, samples // PAIRED)
    def _(it):
        dn_copy(0, it, down_id).wait()
        dn_copy(1, it, up_id).wait()

    def atom_step(c, gain_acc):
        some = pl.ds(c * GROUP, GROUP)
        flat = (GROUP * count, width)
        cube = (GROUP, count, width)
        grad = (dn_own[some] + dn_in[0, some].astype(F32) + dn_in[1, some].astype(F32)).reshape(flat)
        xhat = xhat_s[some].reshape(flat)
        back = norm_back(grad, again, xhat, rstd_s[some].reshape(GROUP * count, 1))
        grad_atoms[some] = cot[some].astype(F32) + back.reshape(cube)
        return gain_acc + fold8(grad * xhat)

    again_acc = lax.fori_loop(0, samples // GROUP, atom_step, jnp.zeros((8, width), F32))

    @pl.loop(1, n_col)
    def _(d):
        peer = col_peer(d)
        cb_copy(peer, peer).wait()

    whole = cb[0]
    for c in range(1, n_col):
        whole = whole + cb[c]
    ag[row] = whole.astype(BF16)

    def ag_copy(peer, slot):
        return pltpu.make_async_remote_copy(
            src_ref=ag.at[row], dst_ref=ag.at[slot], send_sem=ag_ss.at[peer],
            recv_sem=ag_rs.at[slot], device_id=(peer, col), device_id_type=MESH)

    small = [jnp.sum(again_acc, axis=0, keepdims=True), jnp.sum(pgain_acc, axis=0, keepdims=True)]
    for h in range(heads):
        small.append(jnp.sum(w_acc[h * band : (h + 1) * band], axis=0, keepdims=True))
    small.append(jnp.zeros((8 - len(small), width), F32))
    sm[row] = jnp.concatenate(small, axis=0)

    def sm_copy(peer, slot):
        return pltpu.make_async_remote_copy(
            src_ref=sm.at[row], dst_ref=sm.at[slot], send_sem=sm_ss.at[peer],
            recv_sem=sm_rs.at[slot], device_id=(peer, col), device_id_type=MESH)

    @pl.loop(1, n_row)
    def _(d):
        sm_copy(row_peer(d), row).start()
        ag_copy(row_peer(d), row).start()

    @pl.loop(1, n_row)
    def _(d):
        peer = row_peer(d)
        sm_copy(peer, peer).wait()

    small_part = sm[0]
    for r in range(1, n_row):
        small_part = small_part + sm[r]
    sc[col] = small_part

    def sc_copy(peer, slot):
        return pltpu.make_async_remote_copy(
            src_ref=sc.at[col], dst_ref=sc.at[slot], send_sem=sc_ss.at[peer],
            recv_sem=sc_rs.at[slot], device_id=(row, peer), device_id_type=MESH)

    @pl.loop(1, n_col)
    def _(d):
        sc_copy(col_peer(d), col).start()

    @pl.loop(1, n_row)
    def _(d):
        peer = row_peer(d)
        ag_copy(peer, peer).wait()

    for p in range(4):
        grad_w[p] = ag[p * per : (p + 1) * per].reshape(width, width).astype(F32)

    @pl.loop(1, n_col)
    def _(d):
        peer = col_peer(d)
        sc_copy(peer, peer).wait()

    sums = sc[0]
    for c in range(1, n_col):
        sums = sums + sc[c]
    grad_again[...] = sums[0:1]
    grad_pgain[...] = sums[1:2]
    grad_pweight[...] = sums[2 : 2 + heads]


def per_device(
    n_row, n_col,
    pair_trunk, pair_gain, pair_weight, atom_features, atom_gain, attn_weights, token_atoms,
    window_starts, out_cotangent,
):
    band, cols, width = pair_trunk.shape
    samples, count, _ = atom_features.shape
    heads = pair_weight.shape[0]
    total = cols * n_col
    lanes = max(128, heads * band)
    ext = count + WINDOW
    half = WINDOW // 2
    hq = heads * count
    share = 4 * width // n_row
    vmem = pl.BlockSpec(memory_space=pltpu.VMEM)
    smem = pl.BlockSpec(memory_space=pltpu.SMEM)
    dma = pltpu.SemaphoreType.DMA
    steps = samples // PAIRED
    scratch = [
        ((2, samples, count, width), BF16),
        ((samples, count, width), BF16),
        ((samples, ext, width), BF16),
        ((samples, ext, width), BF16),
        ((samples, ext, width), BF16),
        ((samples, count, width), F32),
        ((samples, count, 1), F32),
        ((samples, count, width), BF16),
        ((samples, count, width), BF16),
        ((samples, count, width), BF16),
        ((samples, ext, 2 * width), BF16),
        ((samples, count, width), F32),
        ((2, samples, half, width), BF16),
        ((2, samples, half, width), BF16),
        ((ext, hq), F32),
        ((ext, hq), F32),
        ((ext, total), BF16),
        ((hq, lanes), BF16),
        ((hq, width), BF16),
        ((lanes, width), BF16),
        ((band, cols, width), F32),
        ((band, cols, 1), F32),
        ((n_col, cols, lanes), BF16),
        ((n_col, cols, lanes), BF16),
        ((n_col, cols, lanes), BF16),
        ((n_row, share, width), BF16),
        ((n_row, share, width), BF16),
        ((n_col, share, width), F32),
        ((n_row, share, width), BF16),
        ((n_row, 8, width), F32),
        ((n_col, 8, width), F32),
    ]
    sems = [(2,), (2,), (n_col,), (n_col,), (2, steps), (2, steps), (n_col,), (n_col,),
            (n_row,), (n_row,), (n_col,), (n_col,), (n_row,), (n_row,), (n_row,), (n_row,),
            (n_col,), (n_col,)]
    outs = pl.pallas_call(
        functools.partial(kernel, n_row, n_col),
        out_shape=[
            jax.ShapeDtypeStruct((samples, count, width), BF16),
            jax.ShapeDtypeStruct((samples, count, width), F32),
            jax.ShapeDtypeStruct((band, cols, width), BF16),
            jax.ShapeDtypeStruct((4, width, width), F32),
            jax.ShapeDtypeStruct((1, width), F32),
            jax.ShapeDtypeStruct((heads, width), F32),
            jax.ShapeDtypeStruct((1, width), F32),
        ],
        in_specs=[vmem] * 7 + [smem, vmem],
        out_specs=[vmem] * 7,
        scratch_shapes=[pltpu.VMEM(shape, kind) for shape, kind in scratch]
        + [dma(shape) for shape in sems],
        compiler_params=pltpu.CompilerParams(
            collective_id=0, has_side_effects=True, vmem_limit_bytes=48 << 20),
    )(
        pair_trunk, pair_gain.reshape(1, width), pair_weight, atom_features,
        atom_gain.reshape(1, width), attn_weights, token_atoms, window_starts, out_cotangent,
    )
    return (outs[0], outs[1], outs[2], outs[3], outs[4].reshape(width), outs[5],
            outs[6].reshape(width))


def solution(mesh):
    atoms_at = P(None, ("row", "col"), None)
    pairs_at = P("row", "col", None)
    return jax.shard_map(
        functools.partial(per_device, mesh.shape["row"], mesh.shape["col"]),
        mesh=mesh,
        in_specs=(pairs_at, P(), P(), atoms_at, P(), P(), P(), P(("row", "col")), atoms_at),
        out_specs=(atoms_at, atoms_at, pairs_at, P(), P(), P(), P()),
        check_vma=False,
    )
```

time: 422 us -> 52.2 us (0.12)
  local copies, waits for them, and re-layouts: 151 us -> 9.81 us
  waiting for transfers between devices: 88.1 us -> 0 us
  other arithmetic: 84.6 us -> 0 us
  blocking collectives: 49.2 us -> 0 us
  Pallas kernels: 0 us -> 41.4 us
  matrix products: 21 us -> 0 us
  between operations: 16.2 us -> 0.69 us
  starting transfers between devices: 9.88 us -> 0 us
    gather x5 -> x0, local copies, waits for them, and re-layouts: 94.8 us -> none  [the longest x2 91.3 us: attend(): bias_window[:, query_tok[:, :, None], key_tok[:, None, :]]]
    psum x1 -> x0, waiting for transfers between devices: 82.4 us -> none  [per_device(): lax.psum((grad_weights, grad_atom_gain, grad_pair_weight, grad_pair_gain)...]
    unnamed x4 -> x0, other arithmetic: 53.6 us -> none
    psum x1 -> x0, blocking collectives: 46 us -> none  [per_device(): lax.psum((grad_weights, grad_atom_gain, grad_pair_weight, grad_pair_gain)...]
    pallas_call x0 -> x1, Pallas kernels: none -> 41.4 us  [per_device(): pl.pallas_call(functools.partial(kernel, n_row, n_col), out_shape=[jax.Sh...]
    scatter-add x9 -> x0, local copies, waits for them, and re-layouts: 24.8 us -> none
    dot_general x14 -> x0, matrix products: 17.9 us -> none  [the longest x3 6.66 us: block_attention(): jnp.einsum('shqk,skhd->sqhd', probs, v_heads, preferred_element_type=jnp....]
    scatter-add x4 -> x0, other arithmetic: 14.2 us -> none
  transfers between devices with their start and end apart: 6 -> 0, of which waited for: 2 -> 0; matrix products, arithmetic and copies ran while one was open for 26% -> 0% of each run, Pallas kernels for 0% -> 0%
where the time goes in v1:
time: 52.2 us; the launch traced here: 51.9 us
  Pallas kernels  41.4 us (79%)
  local copies, waits for them, and re-layouts  9.81 us (19%)
  between operations  0.69 us (1%)
    pallas_call x1, Pallas kernels, per_device(): pl.pallas_call(functools.partial(kernel, n_row, n_col), out_shape=[jax.Sh...  41.4 us
    unnamed x25, local copies, waits for them, and re-layouts  9.81 us

profile of v1, /device:TPU:0, one launch (start us, length us, event | category | flops | bytes accessed | tf_op | source)
XLA Modules:
  0.0 51.9 jit_solution(17982088089457022536)
XLA Ops:
  0.6 0.0 copy-start.7
  0.6 0.0 copy-start.8
  0.7 0.0 copy-start.5
  0.7 0.0 copy-start.6
  0.7 0.6 %copy-done.7 = f32[128]{0:T(128)S(1)} copy-done((f32[128]{0:T(128)S(1)}, f32[128]{0:T(128)}, u32[]{:S(2)}) %copy-start.7) | copy-done | bytes 536
  1.3 0.0 copy-done.8
  1.3 0.0 copy-done.5
  1.3 0.0 copy-done.6
  1.4 0.0 copy-start
  1.4 1.0 %copy-done = bf16[16,128,128]{2,1,0:T(8,128)(2,1)S(1)} copy-done((bf16[16,128,128]{2,1,0:T(8,128)(2,1)S(1)}, bf16[16,128,128]{2,1,0:T(8,128)(2,1)}, u32[]{:S(2)}) %copy-start) | copy-done | bytes 524312
  2.4 0.0 copy-start.1
  2.4 0.9 %copy-done.1 = bf16[16,64,128]{2,1,0:T(8,128)(2,1)S(1)} copy-done((bf16[16,64,128]{2,1,0:T(8,128)(2,1)S(1)}, bf16[16,64,128]{2,1,0:T(8,128)(2,1)}, u32[]{:S(2)}) %copy-start.1) | copy-done | bytes 262168
  3.3 0.0 copy-start.2
  3.3 0.9 %copy-done.2 = bf16[16,64,128]{2,1,0:T(8,128)(2,1)S(1)} copy-done((bf16[16,64,128]{2,1,0:T(8,128)(2,1)S(1)}, bf16[16,64,128]{2,1,0:T(8,128)(2,1)}, u32[]{:S(2)}) %copy-start.2) | copy-done | bytes 262168
  4.3 0.0 copy-start.3
  4.3 0.9 %copy-done.3 = bf16[4,128,128]{2,1,0:T(8,128)(2,1)S(1)} copy-done((bf16[4,128,128]{2,1,0:T(8,128)(2,1)S(1)}, bf16[4,128,128]{2,1,0:T(8,128)(2,1)}, u32[]{:S(2)}) %copy-start.3) | copy-done | bytes 131096
  5.2 0.0 copy-start.4
  5.2 0.7 %copy-done.4 = s32[16,16]{1,0:T(8,128)S(1)} copy-done((s32[16,16]{1,0:T(8,128)S(1)}, s32[16,16]{1,0:T(8,128)}, u32[]{:S(2)}) %copy-start.4) | copy-done | bytes 1048
  5.9 41.4 %shard_map.144 = (bf16[16,64,128]{2,1,0:T(8,128)(2,1)S(1)}, f32[16,64,128]{2,1,0:T(8,128)S(1)}, bf16[16,128,128]{2,1,0:T(8,128)(2,1)S(1)}, f32[4,128,128]{2,1,0:...) custom-call(bf16[16,128,128]{2,1,0:T(8,128)(2,1)S(1)} %copy-done, ...), custom_call_target="tpu_custom_call" | custom-call | tf_op jit(solution)/shard_map/pallas_call | solution.py:493
  47.3 0.7 %copy.23 = bf16[16,64,128]{2,1,0:T(8,128)(2,1)} copy(bf16[16,64,128]{2,1,0:T(8,128)(2,1)S(1)} %get-tuple-element.28) | data formatting | bytes 524288
  48.0 0.8 %copy.24 = f32[16,64,128]{2,1,0:T(8,128)} copy(f32[16,64,128]{2,1,0:T(8,128)S(1)} %get-tuple-element.29) | data formatting | bytes 1048576
  48.8 0.8 %copy.25 = bf16[16,128,128]{2,1,0:T(8,128)(2,1)} copy(bf16[16,128,128]{2,1,0:T(8,128)(2,1)S(1)} %get-tuple-element.30) | data formatting | bytes 1048576
  49.6 0.7 %copy.26 = f32[4,128,128]{2,1,0:T(8,128)} copy(f32[4,128,128]{2,1,0:T(8,128)S(1)} %get-tuple-element.31) | data formatting | bytes 524288
  50.3 0.5 copy.27
  50.8 0.6 %copy.28 = f32[4,128]{1,0:T(4,128)} copy(f32[4,128]{1,0:T(4,128)S(1)} %get-tuple-element.33) | data formatting | bytes 4096
  51.4 0.5 copy.29
Async XLA Ops:
  0.6 0.7 %copy-start.7 = (f32[128]{0:T(128)S(1)}, f32[128]{0:T(128)}, u32[]{:S(2)}) copy-start(f32[128]{0:T(128)} %param.13) | copy-start | bytes 1540
  0.6 0.7 %copy-start.8 = (s32[2]{0:T(128)S(1)}, s32[2]{0:T(128)}, u32[]{:S(2)}) copy-start(s32[2]{0:T(128)} %starts.1) | copy-start | bytes 28
  0.7 0.7 %copy-start.5 = (bf16[4,128]{1,0:T(4,128)(2,1)S(1)}, bf16[4,128]{1,0:T(4,128)(2,1)}, u32[]{:S(2)}) copy-start(bf16[4,128]{1,0:T(4,128)(2,1)} %pair_weight.1) | copy-start | bytes 3076
  0.7 0.7 %copy-start.6 = (f32[128]{0:T(128)S(1)}, f32[128]{0:T(128)}, u32[]{:S(2)}) copy-start(f32[128]{0:T(128)} %param.10) | copy-start | bytes 1540
  1.4 1.0 %copy-start = (bf16[16,128,128]{2,1,0:T(8,128)(2,1)S(1)}, bf16[16,128,128]{2,1,0:T(8,128)(2,1)}, u32[]{:S(2)}) copy-start(bf16[16,128,128]{2,1,0:T(8,128)(2,1)} %trunk.1) | copy-start | bytes 1572868
  2.4 0.9 %copy-start.1 = (bf16[16,64,128]{2,1,0:T(8,128)(2,1)S(1)}, bf16[16,64,128]{2,1,0:T(8,128)(2,1)}, u32[]{:S(2)}) copy-start(bf16[16,64,128]{2,1,0:T(8,128)(2,1)} %atoms.1) | copy-start | bytes 786436
  3.3 0.9 %copy-start.2 = (bf16[16,64,128]{2,1,0:T(8,128)(2,1)S(1)}, bf16[16,64,128]{2,1,0:T(8,128)(2,1)}, u32[]{:S(2)}) copy-start(bf16[16,64,128]{2,1,0:T(8,128)(2,1)} %cot.1) | copy-start | bytes 786436
  4.3 0.9 %copy-start.3 = (bf16[4,128,128]{2,1,0:T(8,128)(2,1)S(1)}, bf16[4,128,128]{2,1,0:T(8,128)(2,1)}, u32[]{:S(2)}) copy-start(bf16[4,128,128]{2,1,0:T(8,128)(2,1)} %weights.1) | copy-start | bytes 393220
  5.2 0.7 %copy-start.4 = (s32[16,16]{1,0:T(8,128)S(1)}, s32[16,16]{1,0:T(8,128)}, u32[]{:S(2)}) copy-start(s32[16,16]{1,0:T(8,128)} %token_atoms.1) | copy-start | bytes 3076

commit v2 on v1

--- a/solution.py
+++ b/solution.py
@@ -49,12 +49,13 @@
 
 def kernel(
     n_row, n_col,
-    trunk, pair_gain, pair_weight, atoms, atom_gain, weights, token_atoms, starts, cot,
+    trunk_h, pgain_h, pweight_h, atoms_h, again_h, weights_h, tokens_h, starts_h, cot_h,
     updated, grad_atoms, grad_pair, grad_w, grad_again, grad_pweight, grad_pgain,
+    trunk, pair_gain, pair_weight, atoms, atom_gain, weights, token_atoms, cot, starts,
     halo, q_s, k_ext, v_ext, n_ext, xhat_s, rstd_s, gmix, mixed_s, dq_s, dkv_s,
     dn_own, dn_out, dn_in, tile, dt_acc, ok_s, oq_s, hmask_s, wrep_s, pxhat, prstd,
     bias_all, g_out, g_in, rs_out, rs_in, cb, ag, sm, sc,
-    halo_ss, halo_rs, bias_ss, bias_rs, dn_ss, dn_rs, g_ss, g_rs,
+    in_s, halo_ss, halo_rs, bias_ss, bias_rs, dn_ss, dn_rs, g_ss, g_rs,
     rs_ss, rs_rs, cb_ss, cb_rs, ag_ss, ag_rs, sm_ss, sm_rs, sc_ss, sc_rs,
 ):
     row = lax.axis_index("row")
@@ -84,6 +85,13 @@
     def col_peer(d):
         return lax.rem(col + d, n_col)
 
+    loads = [
+        pltpu.make_async_copy(source, target, in_s.at[n])
+        for n, (source, target) in enumerate((
+            (trunk_h, trunk), (pgain_h, pair_gain), (pweight_h, pair_weight),
+            (again_h, atom_gain), (atoms_h, atoms), (weights_h, weights), (cot_h, cot),
+            (tokens_h, token_atoms), (starts_h, starts)))
+    ]
     barrier = pltpu.get_barrier_semaphore()
     pl.semaphore_signal(barrier, inc=1, device_id=up_id, device_id_type=MESH)
     pl.semaphore_signal(barrier, inc=1, device_id=down_id, device_id_type=MESH)
@@ -96,8 +104,55 @@
     def _(d):
         pl.semaphore_signal(barrier, inc=1, device_id=(row, col_peer(d)), device_id_type=MESH)
 
+    for copy in loads:
+        copy.start()
+    pl.semaphore_wait(barrier, n_row + n_col)
+
+    def halo_copy(d, it, where):
+        some = pl.ds(it * PAIRED, PAIRED)
+        return pltpu.make_async_remote_copy(
+            src_ref=atoms_h.at[some], dst_ref=halo.at[d, some], send_sem=halo_ss.at[d, it],
+            recv_sem=halo_rs.at[d, it], device_id=where, device_id_type=MESH)
+
+    @pl.loop(0, samples // PAIRED)
+    def _(it):
+        halo_copy(0, it, up_id).start()
+        halo_copy(1, it, down_id).start()
+
+    for copy in loads[:4]:
+        copy.wait()
     again = atom_gain[...]
     pgain = pair_gain[...]
+
+    lane_row = iota((lanes, width), 0)
+    wrep = jnp.zeros((lanes, width), F32)
+    for h in range(heads):
+        wrep = jnp.where(lane_row // band == h, pair_weight[h : h + 1, :].astype(F32), wrep)
+    wrep_s[...] = wrep.astype(BF16)
+
+    def pair_rows(i):
+        return jnp.where(lane_row % band == i, wrep_s[...].astype(F32), 0.0).astype(BF16)
+
+    def forward_step(i, acc):
+        xhat, rstd = normalised(trunk[i])
+        pxhat[i] = xhat
+        prstd[i] = rstd
+        return acc + dot((xhat * pgain).astype(BF16), pair_rows(i), NT)
+
+    bias = lax.fori_loop(0, band, forward_step, jnp.zeros((cols, lanes), F32), unroll=2)
+    bias_all[col] = bias.astype(BF16)
+
+    def bias_copy(peer, slot):
+        return pltpu.make_async_remote_copy(
+            src_ref=bias_all.at[col], dst_ref=bias_all.at[slot], send_sem=bias_ss.at[peer],
+            recv_sem=bias_rs.at[slot], device_id=(row, peer), device_id_type=MESH)
+
+    @pl.loop(1, n_col)
+    def _(d):
+        bias_copy(col_peer(d), col).start()
+
+    for copy in loads[4:]:
+        copy.wait()
 
     wqkv = jnp.concatenate([weights[0], weights[1], weights[2]], axis=1)
     wkv = jnp.concatenate([weights[1], weights[2]], axis=1)
@@ -118,44 +173,6 @@
         v_ext[some, half : half + count] = proj[:, 2 * width :].reshape(cube)
         gmix[some] = dot(cot[some].reshape(flat), weights[3], NT).astype(BF16).reshape(cube)
 
-    pl.semaphore_wait(barrier, n_row + n_col)
-
-    def halo_copy(d, where):
-        return pltpu.make_async_remote_copy(
-            src_ref=atoms, dst_ref=halo.at[d], send_sem=halo_ss.at[d], recv_sem=halo_rs.at[d],
-            device_id=where, device_id_type=MESH)
-
-    halos = [halo_copy(0, up_id), halo_copy(1, down_id)]
-    for copy in halos:
-        copy.start()
-
-    lane_row = iota((lanes, width), 0)
-    wrep = jnp.zeros((lanes, width), F32)
-    for h in range(heads):
-        wrep = jnp.where(lane_row // band == h, pair_weight[h : h + 1, :].astype(F32), wrep)
-    wrep_s[...] = wrep.astype(BF16)
-
-    def pair_rows(i):
-        return jnp.where(lane_row % band == i, wrep_s[...].astype(F32), 0.0).astype(BF16)
-
-    def forward_step(i, acc):
-        xhat, rstd = normalised(trunk[i])
-        pxhat[i] = xhat
-        prstd[i] = rstd
-        return acc + dot((xhat * pgain).astype(BF16), pair_rows(i), NT)
-
-    bias = lax.fori_loop(0, band, forward_step, jnp.zeros((cols, lanes), F32), unroll=2)
-    bias_all[col] = bias.astype(BF16)
-
-    def bias_copy(peer, slot):
-        return pltpu.make_async_remote_copy(
-            src_ref=bias_all.at[col], dst_ref=bias_all.at[slot], send_sem=bias_ss.at[peer],
-            recv_sem=bias_rs.at[slot], device_id=(row, peer), device_id_type=MESH)
-
-    @pl.loop(1, n_col)
-    def _(d):
-        bias_copy(col_peer(d), col).start()
-
     table = token_atoms[...].astype(F32).astype(BF16)
 
     def bounds(size, token_of, band_of, band_row):
@@ -182,22 +199,6 @@
     hmask_s[...] = jnp.where(
         iota((hq, width), 0) // count == iota((hq, width), 1) // head_dim, 1.0, 0.0).astype(BF16)
 
-    for d, copy in enumerate(halos):
-        copy.wait()
-        base = d * (half + count)
-
-        @pl.loop(0, samples // GROUP)
-        def _(c, d=d, base=base):
-            some = pl.ds(c * GROUP, GROUP)
-            cube = (GROUP, half, width)
-            side = halo[d, some]
-            xhat, _r = normalised(side.reshape(GROUP * half, width))
-            normed = (xhat * again).astype(BF16)
-            proj = dot(normed, wkv, NN).astype(BF16)
-            n_ext[some, base : base + half] = normed.reshape(cube)
-            k_ext[some, base : base + half] = proj[:, :width].reshape(cube)
-            v_ext[some, base : base + half] = proj[:, width:].reshape(cube)
-
     @pl.loop(1, n_col)
     def _(d):
         peer = col_peer(d)
@@ -231,6 +232,18 @@
 
     @pl.loop(0, samples // PAIRED)
     def _(it):
+        halo_copy(0, it, up_id).wait()
+        halo_copy(1, it, down_id).wait()
+        some = pl.ds(it * PAIRED, PAIRED)
+        cube = (PAIRED, half, width)
+        for d in range(2):
+            base = d * (half + count)
+            xhat, _r = normalised(halo[d, some].reshape(PAIRED * half, width))
+            normed = (xhat * again).astype(BF16)
+            proj = dot(normed, wkv, NN).astype(BF16)
+            n_ext[some, base : base + half] = normed.reshape(cube)
+            k_ext[some, base : base + half] = proj[:, :width].reshape(cube)
+            v_ext[some, base : base + half] = proj[:, width:].reshape(cube)
         added = None
         for u in range(PAIRED):
             s = it * PAIRED + u
@@ -436,6 +449,18 @@
     grad_pweight[...] = sums[2 : 2 + heads]
 
 
+def handover(*refs):
+    count = (len(refs) - 1) // 2
+    sems = refs[-1]
+    copies = [
+        pltpu.make_async_copy(refs[n], refs[count + n], sems.at[n]) for n in range(count)
+    ]
+    for copy in copies:
+        copy.start()
+    for copy in copies:
+        copy.wait()
+
+
 def per_device(
     n_row, n_col,
     pair_trunk, pair_gain, pair_weight, atom_features, atom_gain, attn_weights, token_atoms,
@@ -451,10 +476,16 @@
     hq = heads * count
     share = 4 * width // n_row
     vmem = pl.BlockSpec(memory_space=pltpu.VMEM)
-    smem = pl.BlockSpec(memory_space=pltpu.SMEM)
+    anywhere = pl.BlockSpec(memory_space=pl.ANY)
     dma = pltpu.SemaphoreType.DMA
     steps = samples // PAIRED
-    scratch = [
+    hbm = pl.BlockSpec(memory_space=pltpu.HBM)
+    args = [
+        pair_trunk, pair_gain.reshape(1, width), pair_weight, atom_features,
+        atom_gain.reshape(1, width), attn_weights, token_atoms, window_starts, out_cotangent,
+    ]
+    scratch = [(args[n].shape, args[n].dtype) for n in (0, 1, 2, 3, 4, 5, 6, 8)]
+    later = [
         ((2, samples, count, width), BF16),
         ((samples, count, width), BF16),
         ((samples, ext, width), BF16),
@@ -487,7 +518,7 @@
         ((n_row, 8, width), F32),
         ((n_col, 8, width), F32),
     ]
-    sems = [(2,), (2,), (n_col,), (n_col,), (2, steps), (2, steps), (n_col,), (n_col,),
+    sems = [(9,), (2, steps), (2, steps), (n_col,), (n_col,), (2, steps), (2, steps), (n_col,), (n_col,),
             (n_row,), (n_row,), (n_col,), (n_col,), (n_row,), (n_row,), (n_row,), (n_row,),
             (n_col,), (n_col,)]
     outs = pl.pallas_call(
@@ -501,16 +532,22 @@
             jax.ShapeDtypeStruct((heads, width), F32),
             jax.ShapeDtypeStruct((1, width), F32),
         ],
-        in_specs=[vmem] * 7 + [smem, vmem],
+        in_specs=[hbm] * 9,
         out_specs=[vmem] * 7,
         scratch_shapes=[pltpu.VMEM(shape, kind) for shape, kind in scratch]
+        + [pltpu.SMEM(window_starts.shape, jnp.int32)]
+        + [pltpu.VMEM(shape, kind) for shape, kind in later]
         + [dma(shape) for shape in sems],
         compiler_params=pltpu.CompilerParams(
-            collective_id=0, has_side_effects=True, vmem_limit_bytes=48 << 20),
-    )(
-        pair_trunk, pair_gain.reshape(1, width), pair_weight, atom_features,
-        atom_gain.reshape(1, width), attn_weights, token_atoms, window_starts, out_cotangent,
-    )
+            collective_id=0, has_side_effects=True, vmem_limit_bytes=60 << 20),
+    )(*args)
+    outs = pl.pallas_call(
+        handover,
+        out_shape=[pltpu.HBM(out.shape, out.dtype) for out in outs],
+        in_specs=[anywhere] * 7,
+        out_specs=[anywhere] * 7,
+        scratch_shapes=[dma((7,))],
+    )(*outs)
     return (outs[0], outs[1], outs[2], outs[3], outs[4].reshape(width), outs[5],
             outs[6].reshape(width))
 

time: 52.2 us -> 91.3 us (1.75)
  Pallas kernels: 41.4 us -> 90.5 us
  local copies, waits for them, and re-layouts: 9.81 us -> 0 us
    pallas_call x0 -> x1, Pallas kernels: none -> 48.9 us  [per_device(): pl.pallas_call(handover, out_shape=[pltpu.HBM(out.shape, out.dtype) for o...]
    unnamed x25 -> x0, local copies, waits for them, and re-layouts: 9.81 us -> none
where the time goes in v2:
time: 91.3 us; the launch traced here: 91.2 us
  Pallas kernels  90.5 us (99%)
    pallas_call x1, Pallas kernels, per_device(): pl.pallas_call(handover, out_shape=[pltpu.HBM(out.shape, out.dtype) for o...  48.9 us
    pallas_call x1, Pallas kernels, per_device(): pl.pallas_call(functools.partial(kernel, n_row, n_col), out_shape=[jax.Sh...  41.6 us

profile of v2, /device:TPU:0, one launch (start us, length us, event | category | flops | bytes accessed | tf_op | source)
XLA Modules:
  0.0 91.2 jit_solution(3273811193505778226)
XLA Ops:
  0.6 41.6 %shard_map.144 = (bf16[16,64,128]{2,1,0:T(8,128)(2,1)}, f32[16,64,128]{2,1,0:T(8,128)}, bf16[16,128,128]{2,1,0:T(8,128)(2,1)}, f32[4,128,128]{2,1,0:T(8,128)}, f...) custom-call(bf16[16,128,128]{2,1,0:T(8,128)(2,1)} %trunk_h.1, f32[1,128]{1,0:T(1,128)} %bitcast.4, ...), custom_call_target="tpu_custom_call" | custom-call | tf_op jit(solution)/shard_map/pallas_call | solution.py:524
  42.3 48.9 %shard_map.145 = (bf16[16,64,128]{2,1,0:T(8,128)(2,1)}, f32[16,64,128]{2,1,0:T(8,128)}, bf16[16,128,128]{2,1,0:T(8,128)(2,1)}, f32[4,128,128]{2,1,0:T(8,128)}, f...) custom-call(bf16[16,64,128]{2,1,0:T(8,128)(2,1)} %get-tuple-element.21.refs_0_, ...), custom_call_target="tpu_custom_call" | custom-call | tf_op jit(solution)/shard_map/pallas_call | solution.py:544

commit v3 on v2

--- a/solution.py
+++ b/solution.py
@@ -18,7 +18,7 @@
 TN = (((0,), (0,)), ((), ()))
 MASKED = -1e30
 GROUP = 4
-PAIRED = 2
+PAIRED = 4
 
 
 def dot(a, b, dims):
@@ -450,14 +450,21 @@
 
 
 def handover(*refs):
-    count = (len(refs) - 1) // 2
-    sems = refs[-1]
-    copies = [
-        pltpu.make_async_copy(refs[n], refs[count + n], sems.at[n]) for n in range(count)
+    count = (len(refs) - 2) // 3
+    in_s, out_s = refs[-2:]
+    arriving = [
+        pltpu.make_async_copy(refs[n], refs[2 * count + n], in_s.at[n]) for n in range(count)
     ]
-    for copy in copies:
+    leaving = [
+        pltpu.make_async_copy(refs[2 * count + n], refs[count + n], out_s.at[n])
+        for n in range(count)
+    ]
+    for copy in arriving:
         copy.start()
-    for copy in copies:
+    for n in range(count):
+        arriving[n].wait()
+        leaving[n].start()
+    for copy in leaving:
         copy.wait()
 
 
@@ -546,7 +553,8 @@
         out_shape=[pltpu.HBM(out.shape, out.dtype) for out in outs],
         in_specs=[anywhere] * 7,
         out_specs=[anywhere] * 7,
-        scratch_shapes=[dma((7,))],
+        scratch_shapes=[pltpu.VMEM(out.shape, out.dtype) for out in outs] + [dma((7,)), dma((7,))],
+        compiler_params=pltpu.CompilerParams(vmem_limit_bytes=60 << 20),
     )(*outs)
     return (outs[0], outs[1], outs[2], outs[3], outs[4].reshape(width), outs[5],
             outs[6].reshape(width))

time: 91.3 us -> 41.3 us (0.45)
  Pallas kernels: 90.5 us -> 40.5 us
    pallas_call x1, Pallas kernels: 48.9 us -> 2.3 us  [per_device(): pl.pallas_call(handover, out_shape=[pltpu.HBM(out.shape, out.dtype) for o...]
    pallas_call x1, Pallas kernels: 41.6 us -> 38.2 us  [per_device(): pl.pallas_call(functools.partial(kernel, n_row, n_col), out_shape=[jax.Sh...]
where the time goes in v3:
time: 41.3 us; the launch traced here: 41.1 us
  Pallas kernels  40.5 us (98%)
  between operations  0.64 us (2%)
    pallas_call x1, Pallas kernels, per_device(): pl.pallas_call(functools.partial(kernel, n_row, n_col), out_shape=[jax.Sh...  38.2 us
    pallas_call x1, Pallas kernels, per_device(): pl.pallas_call(handover, out_shape=[pltpu.HBM(out.shape, out.dtype) for o...  2.3 us

profile of v3, /device:TPU:0, one launch (start us, length us, event | category | flops | bytes accessed | tf_op | source)
XLA Modules:
  0.0 41.1 jit_solution(381905508389240887)
XLA Ops:
  0.6 38.2 %shard_map.144 = (bf16[16,64,128]{2,1,0:T(8,128)(2,1)}, f32[16,64,128]{2,1,0:T(8,128)}, bf16[16,128,128]{2,1,0:T(8,128)(2,1)}, f32[4,128,128]{2,1,0:T(8,128)}, f...) custom-call(bf16[16,128,128]{2,1,0:T(8,128)(2,1)} %trunk_h.1, f32[1,128]{1,0:T(1,128)} %bitcast.4, ...), custom_call_target="tpu_custom_call" | custom-call | tf_op jit(solution)/shard_map/pallas_call | solution.py:531
  38.8 2.3 %shard_map.145 = (bf16[16,64,128]{2,1,0:T(8,128)(2,1)}, f32[16,64,128]{2,1,0:T(8,128)}, bf16[16,128,128]{2,1,0:T(8,128)(2,1)}, f32[4,128,128]{2,1,0:T(8,128)}, f...) custom-call(bf16[16,64,128]{2,1,0:T(8,128)(2,1)} %get-tuple-element.21.refs_0_, ...), custom_call_target="tpu_custom_call" | custom-call | tf_op jit(solution)/shard_map/pallas_call | solution.py:551

commit v4 on v3

--- a/solution.py
+++ b/solution.py
@@ -79,6 +79,19 @@
     band_atoms = count * n_col
     first = me * count
 
+    has_up = me < n_dev - 1
+    has_down = me > 0
+
+    @pl.when(me == 0)
+    def _():
+        halo[0] = jnp.zeros(halo.shape[1:], BF16)
+        dn_in[1] = jnp.zeros(dn_in.shape[1:], BF16)
+
+    @pl.when(me == n_dev - 1)
+    def _():
+        halo[1] = jnp.zeros(halo.shape[1:], BF16)
+        dn_in[0] = jnp.zeros(dn_in.shape[1:], BF16)
+
     def row_peer(d):
         return lax.rem(row + d, n_row)
 
@@ -116,8 +129,8 @@
 
     @pl.loop(0, samples // PAIRED)
     def _(it):
-        halo_copy(0, it, up_id).start()
-        halo_copy(1, it, down_id).start()
+        pl.when(has_up)(lambda: halo_copy(0, it, up_id).start())
+        pl.when(has_down)(lambda: halo_copy(1, it, down_id).start())
 
     for copy in loads[:4]:
         copy.wait()
@@ -232,8 +245,10 @@
 
     @pl.loop(0, samples // PAIRED)
     def _(it):
-        halo_copy(0, it, up_id).wait()
-        halo_copy(1, it, down_id).wait()
+        pl.when(has_up)(lambda: halo_copy(0, it, up_id).wait_send())
+        pl.when(has_down)(lambda: halo_copy(0, it, up_id).wait_recv())
+        pl.when(has_down)(lambda: halo_copy(1, it, down_id).wait_send())
+        pl.when(has_up)(lambda: halo_copy(1, it, down_id).wait_recv())
         some = pl.ds(it * PAIRED, PAIRED)
         cube = (PAIRED, half, width)
         for d in range(2):
@@ -271,8 +286,8 @@
             dn_out[1, s] = gn[half + count :].astype(BF16)
             dn_own[s] = gn[half : half + count] + dot(gq, weights[0], NT)
         dt_acc[...] += added
-        dn_copy(0, it, down_id).start()
-        dn_copy(1, it, up_id).start()
+        pl.when(has_down)(lambda: dn_copy(0, it, down_id).start())
+        pl.when(has_up)(lambda: dn_copy(1, it, up_id).start())
 
     by_query = dot(dt_acc[...].astype(BF16), oq_s[...], NN).astype(BF16)
     g_out[...] = dot(ok_s[...], by_query, TN).astype(BF16).reshape(n_col, cols, lanes)
@@ -363,8 +378,10 @@
 
     @pl.loop(0, samples // PAIRED)
     def _(it):
-        dn_copy(0, it, down_id).wait()
-        dn_copy(1, it, up_id).wait()
+        pl.when(has_down)(lambda: dn_copy(0, it, down_id).wait_send())
+        pl.when(has_up)(lambda: dn_copy(0, it, down_id).wait_recv())
+        pl.when(has_up)(lambda: dn_copy(1, it, up_id).wait_send())
+        pl.when(has_down)(lambda: dn_copy(1, it, up_id).wait_recv())
 
     def atom_step(c, gain_acc):
         some = pl.ds(c * GROUP, GROUP)

time: 41.3 us -> 40.6 us (0.983)
  Pallas kernels: 40.5 us -> 39.8 us
    pallas_call x1, Pallas kernels: 38.2 us -> 37.5 us  [per_device(): pl.pallas_call(functools.partial(kernel, n_row, n_col), out_shape=[jax.Sh...]
where the time goes in v4:
time: 40.6 us; the launch traced here: 40.5 us
  Pallas kernels  39.8 us (98%)
  between operations  0.64 us (2%)
    pallas_call x1, Pallas kernels, per_device(): pl.pallas_call(functools.partial(kernel, n_row, n_col), out_shape=[jax.Sh...  37.5 us
    pallas_call x1, Pallas kernels, per_device(): pl.pallas_call(handover, out_shape=[pltpu.HBM(out.shape, out.dtype) for o...  2.3 us

profile of v4, /device:TPU:0, one launch (start us, length us, event | category | flops | bytes accessed | tf_op | source)
XLA Modules:
  0.0 40.5 jit_solution(1213616074782404783)
XLA Ops:
  0.6 37.5 %shard_map.144 = (bf16[16,64,128]{2,1,0:T(8,128)(2,1)}, f32[16,64,128]{2,1,0:T(8,128)}, bf16[16,128,128]{2,1,0:T(8,128)(2,1)}, f32[4,128,128]{2,1,0:T(8,128)}, f...) custom-call(bf16[16,128,128]{2,1,0:T(8,128)(2,1)} %trunk_h.1, f32[1,128]{1,0:T(1,128)} %bitcast.4, ...), custom_call_target="tpu_custom_call" | custom-call | tf_op jit(solution)/shard_map/pallas_call | solution.py:548
  38.2 2.3 %shard_map.145 = (bf16[16,64,128]{2,1,0:T(8,128)(2,1)}, f32[16,64,128]{2,1,0:T(8,128)}, bf16[16,128,128]{2,1,0:T(8,128)(2,1)}, f32[4,128,128]{2,1,0:T(8,128)}, f...) custom-call(bf16[16,64,128]{2,1,0:T(8,128)(2,1)} %get-tuple-element.21.refs_0_, ...), custom_call_target="tpu_custom_call" | custom-call | tf_op jit(solution)/shard_map/pallas_call | solution.py:568
